TPU v7x, 32 devices: a whole 2x2x4 slice. The times are simulated.
32 devices in a mesh: groups: 2 (over x), feat: 16 (over z, y, core).
Axes of the slice: x: 2, y: 2, z: 4, core: 2. Of those that a mesh axis runs over, the one named last changes fastest.
Arguments:
- features: bfloat16 [1024, 8192], P('feat', 'groups'), parts along dimension 1, may hold values from -6 to 6
- weight_self: bfloat16 [1024, 256], replicated, may hold values from -0.1875 to 0.1875
- weight_neighbor: bfloat16 [1024, 256], replicated, may hold values from -0.1875 to 0.1875
- cotangent: bfloat16 [4096, 256], P(('groups', 'feat')), parts along dimension 0, may hold values from -0.25 to 0.25
- source_tiles: int32 [32, 16], P('groups'), parts along dimension 0, may hold values from 0 to 31
- neighbor_slots: int32 [4096, 10], P('groups'), parts along dimension 0, may hold values from 0 to 2047
- neighbor_counts: int32 [4096], P('groups'), parts along dimension 0, may hold values from 1 to 10
Outputs:
- activated: bfloat16 [4096, 256], P(('groups', 'feat')), parts along dimension 0
- grad_self: float32 [2048, 256], P(('groups', 'feat')), parts along dimension 0
- grad_neighbor: float32 [2048, 256], P(('groups', 'feat')), parts along dimension 0
There are 2 independent parts, one for each index of `groups`. A program takes and returns all parts, laid end to end along the dimension named above; an argument that names none is the same for every part. Nothing has to cross between parts.
All inputs are finite; a program needn't handle non-finite values.
Results may differ from a plain program's by a relative error of at most 0.0045.
Values may be sent and summed in bfloat16 or wider, within the bound.
A program may use at most 128 MiB of HBM per device.

v0:
```python
import jax
import jax.numpy as jnp
from jax import lax
from jax.sharding import PartitionSpec as P


def aggregate(features, source_tiles, neighbor_slots, neighbor_counts):
    dst_nodes = neighbor_counts.shape[0]
    fanout = neighbor_slots.shape[1]
    tile_rows = jnp.arange(dst_nodes, dtype=jnp.int32) // 128
    picked = source_tiles[tile_rows[:, None], neighbor_slots // 128]
    sources = picked * 128 + neighbor_slots % 128
    used = jnp.arange(fanout, dtype=jnp.int32)[None, :] < neighbor_counts[:, None]
    scales = jnp.where(used, 1.0, 0.0).astype(jnp.float32) / neighbor_counts[:, None].astype(
        jnp.float32
    )

    def add_slot(column, summed):
        index_col = lax.dynamic_index_in_dim(sources, column, 1, keepdims=False)
        scale_col = lax.dynamic_index_in_dim(scales, column, 1, keepdims=False)
        taken = jnp.take(features, index_col, axis=1).astype(jnp.float32)
        return summed + taken * scale_col[None, :]

    summed = lax.fori_loop(
        0, fanout, add_slot, jnp.zeros((features.shape[0], dst_nodes), jnp.float32)
    )
    return summed.astype(jnp.bfloat16)


def contract_rows(left, right_wide):
    return jnp.dot(
        jnp.transpose(left.astype(jnp.float32)), right_wide, preferred_element_type=jnp.float32
    )


def on_device(
    features, weight_self, weight_neighbor, cotangent, source_tiles, neighbor_slots, neighbor_counts
):
    dst_nodes = neighbor_counts.shape[0]
    own_columns = features[:, :dst_nodes]
    mean_columns = aggregate(features, source_tiles, neighbor_slots, neighbor_counts)
    self_rows, mean_rows = (
        lax.all_to_all(own_columns, "feat", split_axis=1, concat_axis=0, tiled=True),
        lax.all_to_all(mean_columns, "feat", split_axis=1, concat_axis=0, tiled=True),
    )
    wide_self = weight_self.astype(jnp.float32)
    wide_neighbor = weight_neighbor.astype(jnp.float32)
    preact = contract_rows(self_rows, wide_self) + contract_rows(mean_rows, wide_neighbor)
    activated = jax.nn.silu(preact).astype(jnp.bfloat16)
    sig_z = jax.nn.sigmoid(preact)
    grad_preact = (cotangent.astype(jnp.float32) * sig_z * (1.0 + preact * (1.0 - sig_z))).astype(
        jnp.bfloat16
    )
    wide_grad = grad_preact.astype(jnp.float32)
    local_width = features.shape[0]
    term_self = jnp.dot(
        self_rows.astype(jnp.float32), wide_grad, preferred_element_type=jnp.float32
    )
    term_mean = jnp.dot(
        mean_rows.astype(jnp.float32), wide_grad, preferred_element_type=jnp.float32
    )
    whole_self, whole_neighbor = lax.psum((term_self, term_mean), "feat")
    first_row = lax.axis_index("feat") * local_width
    grad_self = lax.dynamic_slice_in_dim(whole_self, first_row, local_width, 0)
    grad_neighbor = lax.dynamic_slice_in_dim(whole_neighbor, first_row, local_width, 0)
    return (activated, grad_self, grad_neighbor)


def solution(mesh):
    in_specs = (
        P("feat", "groups"),
        P(),
        P(),
        P(("groups", "feat"), None),
        P("groups", None),
        P("groups", None),
        P("groups"),
    )
    out_specs = (
        P(("groups", "feat"), None),
        P(("groups", "feat"), None),
        P(("groups", "feat"), None),
    )
    return jax.shard_map(
        on_device, mesh=mesh, in_specs=in_specs, out_specs=out_specs, check_vma=False
    )
```

profile of v0, /device:TPU:0, one launch (start us, length us, event | category | flops | bytes accessed | tf_op | source)
XLA Modules:
  0.0 357.2 jit_solution(1774547478237839600)
XLA Ops:
  7.2 1.8 copy_bitcast_fusion
  9.0 7.6 %all-to-all-start = ((bf16[64,16,128]{2,0,1:T(8,128)(2,1)}), bf16[64,16,128]{2,0,1:T(8,128)(2,1)}, u32[]{:S(2)}, u32[]{:S(2)}) async-start(bf16[64,16,128]{2,0,1:T(8,128)(2,1)} %copy_bitcast_fusion), calls=%async_computation | async-start | bytes 524288 | tf_op jit(solution)/shard_map/all_to_all | solution.py:43
  16.6 1.3 copy.35
  18.3 1.0 copy-done.4
  19.3 0.9 fusion.4
  20.2 0.8 reshape.53
  21.0 131.4 %gather_fusion.1 = s32[20480]{0:T(1024)S(1)} fusion(s32[16,16]{1,0:T(8,128)S(1)} %copy-done.1, s32[20480]{0:T(1024)S(1)} %reshape.53), kind=kCustom, calls=%fused_computation.1 | custom fusion | bytes 327680 | tf_op jit(solution)/shard_map/gather | solution.py:11
  152.5 2.0 reshape.60
  154.5 2.7 fusion
  157.2 1.6 copy.34
  158.9 70.3 %while.14 = (s32[]{:T(128)}, f32[64,2048]{0,1:T(8,128)S(1)}, s32[2048,10]{0,1:T(8,128)S(1)}, bf16[64,4096]{0,1:T(8,128)(2,1)S(1)}, f32[2048,10]{0,1:T(8,128)S(1)}, /*index=5*/s32[]{:T(128)}, s32[]{:T(128)}) while((s32[]{:T(128)}, f32[64,2048]{0,1:T(8,128)S(1)}, s32[2048,10]{0,1:T(8,128)S(1)}, bf16[64,4096]{0,1:T(8,128)(2,1)S(1)}, ...), condition=%wide.region_1.2_spmd.clone, body=%wide.region_0.1_spmd.clone.sunk | while | flops 669699 | bytes 1904735 | solution.py:24
  159.0 6.2 %gather_fusion = bf16[2048,64]{1,0:T(8,128)(2,1)S(1)} fusion(bf16[64,4096]{0,1:T(8,128)(2,1)S(1)} %get-tuple-element.216, s32[2048]{0:T(1024)S(1)} %broadcast_clamp_fusion.2), kind=kCustom, calls=%fused_computation.clone.clone.1 | custom fusion | bytes 532480 | tf_op jit(solution)/shard_map/while/body/eval_jaxpr/jit(_take)/gather | solution.py:21
  165.2 0.7 bitcast_add_fusion.2
  166.0 6.2 %gather_fusion = bf16[2048,64]{1,0:T(8,128)(2,1)S(1)} fusion(bf16[64,4096]{0,1:T(8,128)(2,1)S(1)} %get-tuple-element.216, s32[2048]{0:T(1024)S(1)} %broadcast_clamp_fusion.2), kind=kCustom, calls=%fused_computation.clone.clone.1 | custom fusion | bytes 532480 | tf_op jit(solution)/shard_map/while/body/eval_jaxpr/jit(_take)/gather | solution.py:21
  173.0 6.2 %gather_fusion = bf16[2048,64]{1,0:T(8,128)(2,1)S(1)} fusion(bf16[64,4096]{0,1:T(8,128)(2,1)S(1)} %get-tuple-element.216, s32[2048]{0:T(1024)S(1)} %broadcast_clamp_fusion.2), kind=kCustom, calls=%fused_computation.clone.clone.1 | custom fusion | bytes 532480 | tf_op jit(solution)/shard_map/while/body/eval_jaxpr/jit(_take)/gather | solution.py:21
  180.1 6.2 %gather_fusion = bf16[2048,64]{1,0:T(8,128)(2,1)S(1)} fusion(bf16[64,4096]{0,1:T(8,128)(2,1)S(1)} %get-tuple-element.216, s32[2048]{0:T(1024)S(1)} %broadcast_clamp_fusion.2), kind=kCustom, calls=%fused_computation.clone.clone.1 | custom fusion | bytes 532480 | tf_op jit(solution)/shard_map/while/body/eval_jaxpr/jit(_take)/gather | solution.py:21
  187.1 6.2 %gather_fusion = bf16[2048,64]{1,0:T(8,128)(2,1)S(1)} fusion(bf16[64,4096]{0,1:T(8,128)(2,1)S(1)} %get-tuple-element.216, s32[2048]{0:T(1024)S(1)} %broadcast_clamp_fusion.2), kind=kCustom, calls=%fused_computation.clone.clone.1 | custom fusion | bytes 532480 | tf_op jit(solution)/shard_map/while/body/eval_jaxpr/jit(_take)/gather | solution.py:21
  194.1 6.2 %gather_fusion = bf16[2048,64]{1,0:T(8,128)(2,1)S(1)} fusion(bf16[64,4096]{0,1:T(8,128)(2,1)S(1)} %get-tuple-element.216, s32[2048]{0:T(1024)S(1)} %broadcast_clamp_fusion.2), kind=kCustom, calls=%fused_computation.clone.clone.1 | custom fusion | bytes 532480 | tf_op jit(solution)/shard_map/while/body/eval_jaxpr/jit(_take)/gather | solution.py:21
  201.2 6.2 %gather_fusion = bf16[2048,64]{1,0:T(8,128)(2,1)S(1)} fusion(bf16[64,4096]{0,1:T(8,128)(2,1)S(1)} %get-tuple-element.216, s32[2048]{0:T(1024)S(1)} %broadcast_clamp_fusion.2), kind=kCustom, calls=%fused_computation.clone.clone.1 | custom fusion | bytes 532480 | tf_op jit(solution)/shard_map/while/body/eval_jaxpr/jit(_take)/gather | solution.py:21
  208.2 6.2 %gather_fusion = bf16[2048,64]{1,0:T(8,128)(2,1)S(1)} fusion(bf16[64,4096]{0,1:T(8,128)(2,1)S(1)} %get-tuple-element.216, s32[2048]{0:T(1024)S(1)} %broadcast_clamp_fusion.2), kind=kCustom, calls=%fused_computation.clone.clone.1 | custom fusion | bytes 532480 | tf_op jit(solution)/shard_map/while/body/eval_jaxpr/jit(_take)/gather | solution.py:21
  215.2 6.2 %gather_fusion = bf16[2048,64]{1,0:T(8,128)(2,1)S(1)} fusion(bf16[64,4096]{0,1:T(8,128)(2,1)S(1)} %get-tuple-element.216, s32[2048]{0:T(1024)S(1)} %broadcast_clamp_fusion.2), kind=kCustom, calls=%fused_computation.clone.clone.1 | custom fusion | bytes 532480 | tf_op jit(solution)/shard_map/while/body/eval_jaxpr/jit(_take)/gather | solution.py:21
  222.2 6.2 %gather_fusion = bf16[2048,64]{1,0:T(8,128)(2,1)S(1)} fusion(bf16[64,4096]{0,1:T(8,128)(2,1)S(1)} %get-tuple-element.216, s32[2048]{0:T(1024)S(1)} %broadcast_clamp_fusion.2), kind=kCustom, calls=%fused_computation.clone.clone.1 | custom fusion | bytes 532480 | tf_op jit(solution)/shard_map/while/body/eval_jaxpr/jit(_take)/gather | solution.py:21
  229.3 0.9 copy.37
  230.2 6.0 %all-to-all-start.1 = ((bf16[64,16,128]{2,0,1:T(8,128)(2,1)}), bf16[64,16,128]{2,0,1:T(8,128)(2,1)S(1)}, u32[]{:S(2)}, u32[]{:S(2)}) async-start(bf16[64,16,128]{2,0,1:T(8,128)(2,1)} %copy.37), calls=%async_computation.1 | async-start | bytes 524288 | tf_op jit(solution)/shard_map/all_to_all | solution.py:44
  236.2 1.2 fusion.13
  237.4 8.8 %all-to-all-done.1 = bf16[64,16,128]{2,0,1:T(8,128)(2,1)S(1)} async-done(((bf16[64,16,128]{2,0,1:T(8,128)(2,1)}), bf16[64,16,128]{2,0,1:T(8,128)(2,1)S(1)}, u32[]{:S(2)}, u32[]{:S(2)}) %all-to-all-start.1) | async-done | bytes 262176 | tf_op jit(solution)/shard_map/all_to_all | solution.py:44
  246.2 0.9 multiply_convert_fusion.1
  247.1 1.3 fusion.12
  248.4 2.3 convolution_bitcast_fusion
  250.8 96.4 %all-reduce.3.cloned.1.call-done = (f32[1024,256]{0,1:T(8,128)}, f32[1024,256]{1,0:T(8,128)}) async-done(((f32[1024,256]{0,1:T(8,128)}, f32[1024,256]{1,0:T(8,128)}), (f32[1024,256]{0,1:T(8,128)}, f32[1024,256]{1,0:T(8,128)})) %all-reduce.3.cloned.1.call-update) | async-done | bytes 2097168 | tf_op jit(solution)/shard_map/psum | solution.py:62
  347.2 1.0 constant_dynamic-slice_fusion.2
  348.9 1.5 constant_dynamic-slice_fusion.1
  (71 shorter events, 8.5 us)
Async XLA Ops:
  7.2 239.0 %copy-start = (bf16[1024,256]{1,0:T(8,128)(2,1)S(1)}, bf16[1024,256]{1,0:T(8,128)(2,1)}, u32[]{:S(2)}) copy-start(bf16[1024,256]{1,0:T(8,128)(2,1)} %param.11) | copy-start | bytes 1572868
  7.2 9.4 %copy-start.6 = (bf16[64,4096]{1,0:T(8,128)(2,1)S(1)}, bf16[64,4096]{1,0:T(8,128)(2,1)}, u32[]{:S(2)}) copy-start(bf16[64,4096]{1,0:T(8,128)(2,1)} %param.9) | copy-start | bytes 1572868
  9.0 8.9 %copy-start.9 = (s32[2048,10]{0,1:T(8,128)S(1)}, s32[2048,10]{0,1:T(8,128)}, u32[]{:S(2)}) copy-start(s32[2048,10]{0,1:T(8,128)} %param.14) | copy-start | bytes 245764
  9.0 221.2 %all-to-all-start = ((bf16[64,16,128]{2,0,1:T(8,128)(2,1)}), bf16[64,16,128]{2,0,1:T(8,128)(2,1)}, u32[]{:S(2)}, u32[]{:S(2)}) async-start(bf16[64,16,128]{2,0,1:T(8,128)(2,1)} %copy_bitcast_fusion), calls=%async_computation | async-start | bytes 524288 | tf_op jit(solution)/shard_map/all_to_all | solution.py:43
  18.3 1.0 copy-start.4
  20.2 0.8 copy-start.1
  152.5 2.0 copy-start.5
  154.5 4.4 %copy-start.3 = (f32[64,2048]{0,1:T(8,128)S(1)}, f32[64,2048]{0,1:T(8,128)}, u32[]{:S(2)}) copy-start(f32[64,2048]{0,1:T(8,128)} %custom-call.2) | copy-start | bytes 1572868
  157.2 1.6 copy-start.10
  157.2 1.7 copy-start.2
  229.3 6.9 %copy-start.7 = (bf16[1024,256]{1,0:T(8,128)(2,1)S(1)}, bf16[1024,256]{1,0:T(8,128)(2,1)}, u32[]{:S(2)}) copy-start(bf16[1024,256]{1,0:T(8,128)(2,1)} %param.10) | copy-start | bytes 1572868
  230.2 16.0 %all-to-all-start.1 = ((bf16[64,16,128]{2,0,1:T(8,128)(2,1)}), bf16[64,16,128]{2,0,1:T(8,128)(2,1)S(1)}, u32[]{:S(2)}, u32[]{:S(2)}) async-start(bf16[64,16,128]{2,0,1:T(8,128)(2,1)} %copy.37), calls=%async_computation.1 | async-start | bytes 524288 | tf_op jit(solution)/shard_map/all_to_all | solution.py:44
  236.1 11.0 %copy-start.8 = (bf16[128,256]{1,0:T(8,128)(2,1)S(1)}, bf16[128,256]{1,0:T(8,128)(2,1)}, u32[]{:S(2)}) copy-start(bf16[128,256]{1,0:T(8,128)(2,1)} %param.12) | copy-start | bytes 196612
  236.1 111.0 %all-reduce.3.cloned.1.call-start = ((), (), s32[]{:S(2)}) async-start(), calls=%async_computation.2 | async-start | bytes 4194304 | tf_op jit(solution)/shard_map/psum | solution.py:62
Sparse Core Ops, SparseCore 0:
  250.9 96.2 all-reduce.2
where the time goes:
time: 358 us; the launch traced here: 357 us
  local copies, waits for them, and re-layouts  206 us (58%)
  waiting for transfers between devices  105 us (29%)
  between operations  14.2 us (4%)
  starting transfers between devices  13.6 us (4%)
  other arithmetic  11.5 us (3%)
  matrix products  5.75 us (2%)
    gather x1, local copies, waits for them, and re-layouts, aggregate(): picked = source_tiles[tile_rows[:, None], neighbor_slots // 128]  131 us
    psum x1, waiting for transfers between devices, on_device(): whole_self, whole_neighbor = lax.psum((term_self, term_mean), 'feat')  96.4 us
    gather x10, local copies, waits for them, and re-layouts, add_slot(): taken = jnp.take(features, index_col, axis=1).astype(jnp.float32)  61.8 us
    all_to_all x1, waiting for transfers between devices, on_device(): lax.all_to_all(mean_columns, 'feat', split_axis=1, concat_axis=0, tiled=T...  8.75 us
    all_to_all x1, starting transfers between devices, on_device(): lax.all_to_all(own_columns, 'feat', split_axis=1, concat_axis=0, tiled=True)  7.57 us
    add x10, other arithmetic, add_slot(): return summed + taken * scale_col[None, :]  7.18 us
  transfers between devices with their start and end apart: 3, of which 2 were waited for; matrix products, arithmetic and copies ran while one was open for 60% of the time, Pallas kernels for 0%

commit v1 on v0

v1 whole, which is shorter than its diff:
```python
import functools

import jax
import jax.numpy as jnp
from jax import lax
from jax.experimental import pallas as pl
from jax.experimental.pallas import tpu as pltpu
from jax.sharding import PartitionSpec as P

TILE = 128
SUB = 16
MESH = pl.DeviceIdType.MESH


def loop(lo, hi, body):
    def step(i, carry):
        body(i)
        return carry

    if hi > lo:
        lax.fori_loop(lo, hi, step, 0)


def grid_of(n):
    chips = n // 2
    rows = 1
    while rows * rows * 4 <= chips:
        rows *= 2
    return chips // rows, rows


def kernel(
    n,
    feat_ref,
    ws_hbm,
    wn_hbm,
    cot_ref,
    tiles_ref,
    slots_ref,
    counts_ref,
    act_ref,
    gs_ref,
    gn_ref,
    ws_ref,
    wn_ref,
    got_self,
    got_mean,
    mean_buf,
    feat_tiles,
    g_buf,
    grad_acc,
    w_sem,
    self_send,
    self_recv,
    mean_send,
    mean_recv,
    line_send,
    line_recv,
    row_send,
    row_recv,
    core_send,
    core_recv,
):
    me = lax.axis_index("feat")
    lines, rows = grid_of(n)
    core = lax.rem(me, 2)
    row = lax.rem(me // 2, rows)
    line = me // (2 * rows)
    width = feat_ref.shape[0]
    wire = got_self.dtype
    fanout = slots_ref.shape[0]
    listed = tiles_ref.shape[1]

    load_ws = pltpu.make_async_copy(ws_hbm, ws_ref, w_sem.at[0])
    load_wn = pltpu.make_async_copy(wn_hbm, wn_ref, w_sem.at[1])
    load_ws.start()
    load_wn.start()

    barrier = pltpu.get_barrier_semaphore()

    def greet(o):
        pl.semaphore_signal(
            barrier, inc=1, device_id={"feat": lax.rem(me + o, n)}, device_id_type=MESH
        )

    loop(1, n, greet)

    def columns(tile):
        return pl.ds(pl.multiple_of(tile * TILE, TILE), TILE)

    def split(t):
        feat_tiles[t] = feat_ref[:, columns(t)].astype(wire)

    for t in range(feat_ref.shape[1] // TILE):
        split(t)
    got_self[me] = feat_tiles[me]
    pl.semaphore_wait(barrier, n - 1)

    def self_copy(o):
        to = lax.rem(me + o, n)
        return pltpu.make_async_remote_copy(
            src_ref=feat_tiles.at[to],
            dst_ref=got_self.at[me],
            send_sem=self_send.at[o],
            recv_sem=self_recv.at[o],
            device_id={"feat": to},
            device_id_type=MESH,
        )

    def mean_copy(o):
        to = lax.rem(me + o, n)
        return pltpu.make_async_remote_copy(
            src_ref=mean_buf.at[to],
            dst_ref=got_mean.at[me],
            send_sem=mean_send.at[o],
            recv_sem=mean_recv.at[o],
            device_id={"feat": to},
            device_id_type=MESH,
        )

    loop(1, n, lambda o: self_copy(o).start())

    place = (
        lax.broadcasted_iota(jnp.int32, (TILE // SUB, SUB, TILE), 0) * SUB
        + lax.broadcasted_iota(jnp.int32, (TILE // SUB, SUB, TILE), 1)
    ).astype(jnp.int16)
    rank = lax.broadcasted_iota(jnp.int32, (fanout, TILE), 0)

    def mean_of(tile):
        slots = slots_ref[:, columns(tile)]
        counts = counts_ref[:, columns(tile)]
        slots = jnp.where(rank < counts, slots, -1)
        times = jnp.ones((fanout, TILE), jnp.float32)
        for j in range(fanout - 1):
            same = (slots == slots[j : j + 1, :]) & (rank > j)
            times += jnp.where(same, 1.0, 0.0)
        spot = [
            jnp.broadcast_to(slots[k : k + 1, :], (SUB, TILE)).astype(jnp.int16)[None]
            for k in range(fanout)
        ]
        often = [
            jnp.broadcast_to(times[k : k + 1, :], (SUB, TILE)).astype(jnp.bfloat16)[None]
            for k in range(fanout)
        ]
        summed = jnp.zeros((width, TILE), jnp.float32)
        for s in range(0, listed, 2):
            hot = []
            for h in range(2):
                here = place + jnp.int16((s + h) * TILE)
                part = jnp.zeros(here.shape, jnp.bfloat16)
                for k in range(fanout):
                    part = jnp.where(here == spot[k], often[k], part)
                hot.append(part.reshape(TILE, TILE))
            left = [feat_tiles[tiles_ref[tile, s + h]].astype(jnp.bfloat16) for h in range(2)]
            summed += jnp.dot(
                jnp.concatenate(left, axis=1),
                jnp.concatenate(hot, axis=0),
                preferred_element_type=jnp.float32,
            )
        scale = 1.0 / counts.astype(jnp.float32)
        return (summed * scale).astype(jnp.bfloat16).astype(wire)

    def aggregate(o):
        to = lax.rem(me + o, n)
        mean_buf[to] = mean_of(to)
        mean_copy(o).start()

    loop(1, n, aggregate)
    mine = mean_of(me)
    mean_buf[me] = mine
    got_mean[me] = mine

    def project(got, weight):
        x = got[...].reshape(n * width, TILE).astype(jnp.bfloat16)
        return lax.dot_general(
            x, weight[...], (((0,), (0,)), ((), ())), preferred_element_type=jnp.float32
        )

    load_ws.wait()
    loop(1, n, lambda o: self_copy(o).wait_recv())
    preact = project(got_self, ws_ref)
    load_wn.wait()
    loop(1, n, lambda o: mean_copy(o).wait_recv())
    preact += project(got_mean, wn_ref)

    sig = jax.nn.sigmoid(preact)
    cot = cot_ref[...].astype(jnp.float32)
    g_buf[me] = (cot * sig * (1.0 + preact * (1.0 - sig))).astype(jnp.bfloat16)

    def index(l, r, c):
        return (l * rows + r) * 2 + c

    def block(dl, dr, c):
        return index(lax.rem(line - dl + lines, lines), lax.rem(row - dr + rows, rows), c)

    def pass_on(slot, to, send, recv):
        return pltpu.make_async_remote_copy(
            src_ref=g_buf.at[slot],
            dst_ref=g_buf.at[slot],
            send_sem=send,
            recv_sem=recv,
            device_id={"feat": to},
            device_id_type=MESH,
        )

    def line_copy(dl, slot):
        to = index(lax.rem(line + dl, lines), row, core)
        return pass_on(slot, to, line_send.at[dl], line_recv.at[dl])

    def row_copy(dl, dr, slot):
        to = index(line, lax.rem(row + dr, rows), core)
        k = dl * rows + dr
        return pass_on(slot, to, row_send.at[k], row_recv.at[k])

    def core_copy(dl, dr, slot):
        k = dl * rows + dr
        return pass_on(slot, index(line, row, 1 - core), core_send.at[k], core_recv.at[k])

    loop(1, lines, lambda dl: line_copy(dl, me).start())
    loop(1, rows, lambda dr: row_copy(0, dr, me).start())
    core_copy(0, 0, me).start()
    act_ref[...] = (preact * sig).astype(jnp.bfloat16)
    grad_acc[...] = jnp.zeros_like(grad_acc)

    def add_block(slot):
        left = jnp.concatenate(
            [feat_tiles[slot].astype(jnp.bfloat16), mean_buf[slot].astype(jnp.bfloat16)], axis=0
        )
        grad_acc[...] += jnp.dot(left, g_buf[slot], preferred_element_type=jnp.float32)

    add_block(me)

    def from_line(dl):
        slot = block(dl, 0, core)
        line_copy(dl, slot).wait_recv()
        loop(1, rows, lambda dr: row_copy(dl, dr, slot).start())
        core_copy(dl, 0, slot).start()
        add_block(slot)

    loop(1, lines, from_line)

    def from_row(dl):
        def one(dr):
            slot = block(dl, dr, core)
            row_copy(dl, dr, slot).wait_recv()
            core_copy(dl, dr, slot).start()
            add_block(slot)

        loop(1, rows, one)

    loop(0, lines, from_row)

    def from_core(dl):
        def one(dr):
            slot = block(dl, dr, 1 - core)
            core_copy(dl, dr, slot).wait_recv()
            add_block(slot)

        loop(0, rows, one)

    loop(0, lines, from_core)
    gs_ref[...] = grad_acc[:width, :]
    gn_ref[...] = grad_acc[width:, :]

    loop(1, n, lambda o: self_copy(o).wait_send())
    loop(1, n, lambda o: mean_copy(o).wait_send())
    loop(1, lines, lambda dl: line_copy(dl, me).wait_send())

    def finish(dl):
        loop(1, rows, lambda dr: row_copy(dl, dr, block(dl, 0, core)).wait_send())
        loop(0, rows, lambda dr: core_copy(dl, dr, block(dl, dr, core)).wait_send())

    loop(0, lines, finish)


def on_device(
    n, features, weight_self, weight_neighbor, cotangent, source_tiles, neighbor_slots, neighbor_counts
):
    width = features.shape[0]
    hidden = weight_self.shape[1]
    dst_nodes = neighbor_counts.shape[0]
    assert dst_nodes == n * TILE and n % 2 == 0
    lines, rows = grid_of(n)
    wire = jnp.bfloat16 if width % SUB == 0 else jnp.float32
    vmem = pl.BlockSpec(memory_space=pltpu.VMEM)
    smem = pl.BlockSpec(memory_space=pltpu.SMEM)
    anywhere = pl.BlockSpec(memory_space=pl.ANY)
    slab = pltpu.VMEM((n, width, TILE), wire)
    dma = pltpu.SemaphoreType.DMA
    body = functools.partial(kernel, n)
    scratch = [
        pltpu.VMEM(weight_self.shape, jnp.bfloat16),
        pltpu.VMEM(weight_self.shape, jnp.bfloat16),
        slab,
        slab,
        slab,
        pltpu.VMEM((features.shape[1] // TILE, width, TILE), wire),
        pltpu.VMEM((n, TILE, hidden), jnp.bfloat16),
        pltpu.VMEM((2 * width, hidden), jnp.float32),
        dma((2,)),
        dma((n,)),
        dma((n,)),
        dma((n,)),
        dma((n,)),
        dma((lines,)),
        dma((lines,)),
        dma((lines * rows,)),
        dma((lines * rows,)),
        dma((lines * rows,)),
        dma((lines * rows,)),
    ]
    return pl.pallas_call(
        body,
        out_shape=(
            jax.ShapeDtypeStruct(cotangent.shape, jnp.bfloat16),
            jax.ShapeDtypeStruct((width, hidden), jnp.float32),
            jax.ShapeDtypeStruct((width, hidden), jnp.float32),
        ),
        in_specs=[vmem, anywhere, anywhere, vmem, smem, vmem, vmem],
        out_specs=(vmem, vmem, vmem),
        scratch_shapes=scratch,
        compiler_params=pltpu.CompilerParams(
            collective_id=0, has_side_effects=True, vmem_limit_bytes=32 * 1024 * 1024
        ),
        name="sage_layer",
    )(
        features,
        weight_self,
        weight_neighbor,
        cotangent,
        source_tiles,
        jnp.transpose(neighbor_slots),
        neighbor_counts.reshape(1, dst_nodes),
    )


def solution(mesh):
    in_specs = (
        P("feat", "groups"),
        P(),
        P(),
        P(("groups", "feat"), None),
        P("groups", None),
        P("groups", None),
        P("groups"),
    )
    out_specs = (
        P(("groups", "feat"), None),
        P(("groups", "feat"), None),
        P(("groups", "feat"), None),
    )
    return jax.shard_map(
        functools.partial(on_device, mesh.shape["feat"]),
        mesh=mesh,
        in_specs=in_specs,
        out_specs=out_specs,
        check_vma=False,
    )
```

time: 358 us -> 42.5 us (0.12)
  local copies, waits for them, and re-layouts: 206 us -> 8.14 us
  waiting for transfers between devices: 105 us -> 0 us
  Pallas kernels: 0 us -> 33.3 us
  starting transfers between devices: 13.6 us -> 0 us
  between operations: 14.2 us -> 0.66 us
  other arithmetic: 11.5 us -> 0 us
  matrix products: 5.75 us -> 0 us
    gather x11 -> x0, local copies, waits for them, and re-layouts: 193 us -> none  [the longest x1 131 us: aggregate(): picked = source_tiles[tile_rows[:, None], neighbor_slots // 128]]
    psum x1 -> x0, waiting for transfers between devices: 96.4 us -> none  [on_device(): whole_self, whole_neighbor = lax.psum((term_self, term_mean), 'feat')]
    pallas_call x0 -> x1, Pallas kernels: none -> 33.3 us  [on_device(): pl.pallas_call(body, out_shape=(jax.ShapeDtypeStruct(cotangent.shape, jnp...]
    all_to_all x2 -> x0, starting transfers between devices: 13.5 us -> none  [the longest x1 7.57 us: on_device(): lax.all_to_all(own_columns, 'feat', split_axis=1, concat_axis=0, tiled=True)]
    add x11 -> x0, other arithmetic: 9.86 us -> none  [the longest x10 7.18 us: add_slot(): return summed + taken * scale_col[None, :]]
    all_to_all x2 -> x0, waiting for transfers between devices: 8.76 us -> none  [the longest x1 8.75 us: on_device(): lax.all_to_all(mean_columns, 'feat', split_axis=1, concat_axis=0, tiled=T...]
    dot_general x4 -> x0, matrix products: 5.75 us -> none  [the longest x1 2.29 us: on_device(): jnp.dot(self_rows.astype(jnp.float32), wide_grad, preferred_element_type=...]
    unnamed x26 -> x17, local copies, waits for them, and re-layouts: 5.1 us -> 8.14 us
  transfers between devices with their start and end apart: 3 -> 0, of which waited for: 2 -> 0; matrix products, arithmetic and copies ran while one was open for 60% -> 0% of each run, Pallas kernels for 0% -> 0%
where the time goes in v1:
time: 42.5 us; the launch traced here: 42.1 us
  Pallas kernels  33.3 us (78%)
  local copies, waits for them, and re-layouts  8.14 us (19%)
  between operations  0.66 us (2%)
    pallas_call x1, Pallas kernels, on_device(): pl.pallas_call(body, out_shape=(jax.ShapeDtypeStruct(cotangent.shape, jnp...  33.3 us
    unnamed x17, local copies, waits for them, and re-layouts  8.14 us

profile of v1, /device:TPU:0, one launch (start us, length us, event | category | flops | bytes accessed | tf_op | source)
XLA Modules:
  0.0 42.1 jit_solution(12030382879470179678)
XLA Ops:
  0.6 0.0 copy-start
  0.6 1.0 %copy-done = bf16[64,4096]{1,0:T(8,128)(2,1)S(1)} copy-done((bf16[64,4096]{1,0:T(8,128)(2,1)S(1)}, bf16[64,4096]{1,0:T(8,128)(2,1)}, u32[]{:S(2)}) %copy-start) | copy-done | bytes 524312
  1.7 0.0 copy-start.1
  1.7 1.0 %copy-done.1 = bf16[1024,256]{1,0:T(8,128)(2,1)S(1)} copy-done((bf16[1024,256]{1,0:T(8,128)(2,1)S(1)}, bf16[1024,256]{1,0:T(8,128)(2,1)}, u32[]{:S(2)}) %copy-start.1) | copy-done | bytes 524312
  2.7 0.0 copy-start.2
  2.7 1.0 %copy-done.2 = bf16[1024,256]{1,0:T(8,128)(2,1)S(1)} copy-done((bf16[1024,256]{1,0:T(8,128)(2,1)S(1)}, bf16[1024,256]{1,0:T(8,128)(2,1)}, u32[]{:S(2)}) %copy-start.2) | copy-done | bytes 524312
  3.8 0.0 copy-start.3
  3.8 0.9 %copy-done.3 = s32[2048,10]{0,1:T(8,128)S(1)} copy-done((s32[2048,10]{0,1:T(8,128)S(1)}, s32[2048,10]{0,1:T(8,128)}, u32[]{:S(2)}) %copy-start.3) | copy-done | bytes 81944
  4.7 0.0 copy-start.4
  4.7 0.8 %copy-done.4 = bf16[128,256]{1,0:T(8,128)(2,1)S(1)} copy-done((bf16[128,256]{1,0:T(8,128)(2,1)S(1)}, bf16[128,256]{1,0:T(8,128)(2,1)}, u32[]{:S(2)}) %copy-start.4) | copy-done | bytes 65560
  5.5 0.0 copy-start.5
  5.5 0.7 %copy-done.5 = s32[16,16]{1,0:T(8,128)S(1)} copy-done((s32[16,16]{1,0:T(8,128)S(1)}, s32[16,16]{1,0:T(8,128)}, u32[]{:S(2)}) %copy-start.5) | copy-done | bytes 1048
  6.2 0.0 copy-start.6
  6.2 0.7 %copy-done.6 = s32[2048]{0:T(1024)S(1)} copy-done((s32[2048]{0:T(1024)S(1)}, s32[2048]{0:T(1024)}, u32[]{:S(2)}) %copy-start.6) | copy-done | bytes 8216
  6.9 33.3 %sage_layer.1 = (bf16[128,256]{1,0:T(8,128)(2,1)S(1)}, f32[64,256]{1,0:T(8,128)S(1)}, f32[64,256]{1,0:T(8,128)S(1)}) custom-call(bf16[64,4096]{1,0:T(8,128)(2,1)S(1)} %copy-done, bf16[1024,256]{1,0:T(8,128)(2,1)S(1)} %copy-done.1, bf16[1024,256]{1,0:T(8,128)(2,1)S(1)} %copy-done.2, bf16[128,256]{1,0:T(8,128)(2,1)S(1)} %copy-done.4, s32[16,16]{1,0:T(8,128)S(1)} %copy-done.5, ...), custom_call_target="tpu_custom_call" | custom-call | tf_op jit(solution)/shard_map/sage_layer/pallas_call | solution.py:312
  40.2 0.6 %copy.13 = bf16[128,256]{1,0:T(8,128)(2,1)} copy(bf16[128,256]{1,0:T(8,128)(2,1)S(1)} %get-tuple-element.6) | data formatting | bytes 131072
  40.8 0.6 %copy.14 = f32[64,256]{1,0:T(8,128)} copy(f32[64,256]{1,0:T(8,128)S(1)} %get-tuple-element.7) | data formatting | bytes 131072
  41.4 0.6 %copy.15 = f32[64,256]{1,0:T(8,128)} copy(f32[64,256]{1,0:T(8,128)S(1)} %get-tuple-element.8) | data formatting | bytes 131072
Async XLA Ops:
  0.6 1.0 %copy-start = (bf16[64,4096]{1,0:T(8,128)(2,1)S(1)}, bf16[64,4096]{1,0:T(8,128)(2,1)}, u32[]{:S(2)}) copy-start(bf16[64,4096]{1,0:T(8,128)(2,1)} %feat_ref.1) | copy-start | bytes 1572868
  1.7 1.0 %copy-start.1 = (bf16[1024,256]{1,0:T(8,128)(2,1)S(1)}, bf16[1024,256]{1,0:T(8,128)(2,1)}, u32[]{:S(2)}) copy-start(bf16[1024,256]{1,0:T(8,128)(2,1)} %ws_hbm.1) | copy-start | bytes 1572868
  2.7 1.0 %copy-start.2 = (bf16[1024,256]{1,0:T(8,128)(2,1)S(1)}, bf16[1024,256]{1,0:T(8,128)(2,1)}, u32[]{:S(2)}) copy-start(bf16[1024,256]{1,0:T(8,128)(2,1)} %wn_hbm.1) | copy-start | bytes 1572868
  3.8 0.9 %copy-start.3 = (s32[2048,10]{0,1:T(8,128)S(1)}, s32[2048,10]{0,1:T(8,128)}, u32[]{:S(2)}) copy-start(s32[2048,10]{0,1:T(8,128)} %param.12) | copy-start | bytes 245764
  4.7 0.8 %copy-start.4 = (bf16[128,256]{1,0:T(8,128)(2,1)S(1)}, bf16[128,256]{1,0:T(8,128)(2,1)}, u32[]{:S(2)}) copy-start(bf16[128,256]{1,0:T(8,128)(2,1)} %cot_ref.1) | copy-start | bytes 196612
  5.5 0.7 %copy-start.5 = (s32[16,16]{1,0:T(8,128)S(1)}, s32[16,16]{1,0:T(8,128)}, u32[]{:S(2)}) copy-start(s32[16,16]{1,0:T(8,128)} %tiles_ref.1) | copy-start | bytes 3076
  6.2 0.7 %copy-start.6 = (s32[2048]{0:T(1024)S(1)}, s32[2048]{0:T(1024)}, u32[]{:S(2)}) copy-start(s32[2048]{0:T(1024)} %param.13) | copy-start | bytes 24580

commit v2 on v1

--- a/solution.py
+++ b/solution.py
@@ -31,25 +31,30 @@
 
 def kernel(
     n,
-    feat_ref,
+    feat_hbm,
     ws_hbm,
     wn_hbm,
+    cot_hbm,
+    tiles_hbm,
+    slots_hbm,
+    counts_hbm,
+    act_ref,
+    gs_ref,
+    gn_ref,
+    feat_ref,
+    ws_ref,
+    wn_ref,
     cot_ref,
     tiles_ref,
     slots_ref,
     counts_ref,
-    act_ref,
-    gs_ref,
-    gn_ref,
-    ws_ref,
-    wn_ref,
     got_self,
     got_mean,
     mean_buf,
     feat_tiles,
     g_buf,
     grad_acc,
-    w_sem,
+    load_sem,
     self_send,
     self_recv,
     mean_send,
@@ -71,10 +76,22 @@
     fanout = slots_ref.shape[0]
     listed = tiles_ref.shape[1]
 
-    load_ws = pltpu.make_async_copy(ws_hbm, ws_ref, w_sem.at[0])
-    load_wn = pltpu.make_async_copy(wn_hbm, wn_ref, w_sem.at[1])
-    load_ws.start()
-    load_wn.start()
+    loads = [
+        pltpu.make_async_copy(src, dst, load_sem.at[i])
+        for i, (src, dst) in enumerate(
+            [
+                (feat_hbm, feat_ref),
+                (tiles_hbm, tiles_ref),
+                (slots_hbm, slots_ref),
+                (counts_hbm, counts_ref),
+                (ws_hbm, ws_ref),
+                (wn_hbm, wn_ref),
+                (cot_hbm, cot_ref),
+            ]
+        )
+    ]
+    for load in loads:
+        load.start()
 
     barrier = pltpu.get_barrier_semaphore()
 
@@ -91,6 +108,7 @@
     def split(t):
         feat_tiles[t] = feat_ref[:, columns(t)].astype(wire)
 
+    loads[0].wait()
     for t in range(feat_ref.shape[1] // TILE):
         split(t)
     got_self[me] = feat_tiles[me]
@@ -119,6 +137,8 @@
         )
 
     loop(1, n, lambda o: self_copy(o).start())
+    for load in loads[1:4]:
+        load.wait()
 
     place = (
         lax.broadcasted_iota(jnp.int32, (TILE // SUB, SUB, TILE), 0) * SUB
@@ -176,10 +196,10 @@
             x, weight[...], (((0,), (0,)), ((), ())), preferred_element_type=jnp.float32
         )
 
-    load_ws.wait()
+    for load in loads[4:]:
+        load.wait()
     loop(1, n, lambda o: self_copy(o).wait_recv())
     preact = project(got_self, ws_ref)
-    load_wn.wait()
     loop(1, n, lambda o: mean_copy(o).wait_recv())
     preact += project(got_mean, wn_ref)
 
@@ -271,6 +291,17 @@
         loop(0, rows, lambda dr: core_copy(dl, dr, block(dl, dr, core)).wait_send())
 
     loop(0, lines, finish)
+
+
+def write_results(a_ref, b_ref, c_ref, a_out, b_out, c_out, sem):
+    copies = [
+        pltpu.make_async_copy(src, dst, sem.at[i])
+        for i, (src, dst) in enumerate([(a_ref, a_out), (b_ref, b_out), (c_ref, c_out)])
+    ]
+    for copy in copies:
+        copy.start()
+    for copy in copies:
+        copy.wait()
 
 
 def on_device(
@@ -283,21 +314,25 @@
     lines, rows = grid_of(n)
     wire = jnp.bfloat16 if width % SUB == 0 else jnp.float32
     vmem = pl.BlockSpec(memory_space=pltpu.VMEM)
-    smem = pl.BlockSpec(memory_space=pltpu.SMEM)
-    anywhere = pl.BlockSpec(memory_space=pl.ANY)
+    hbm = pl.BlockSpec(memory_space=pltpu.HBM)
     slab = pltpu.VMEM((n, width, TILE), wire)
     dma = pltpu.SemaphoreType.DMA
     body = functools.partial(kernel, n)
     scratch = [
+        pltpu.VMEM(features.shape, jnp.bfloat16),
         pltpu.VMEM(weight_self.shape, jnp.bfloat16),
         pltpu.VMEM(weight_self.shape, jnp.bfloat16),
+        pltpu.VMEM(cotangent.shape, jnp.bfloat16),
+        pltpu.SMEM(source_tiles.shape, jnp.int32),
+        pltpu.VMEM(neighbor_slots.shape[::-1], jnp.int32),
+        pltpu.VMEM((1, dst_nodes), jnp.int32),
         slab,
         slab,
         slab,
         pltpu.VMEM((features.shape[1] // TILE, width, TILE), wire),
         pltpu.VMEM((n, TILE, hidden), jnp.bfloat16),
         pltpu.VMEM((2 * width, hidden), jnp.float32),
-        dma((2,)),
+        dma((7,)),
         dma((n,)),
         dma((n,)),
         dma((n,)),
@@ -309,18 +344,18 @@
         dma((lines * rows,)),
         dma((lines * rows,)),
     ]
-    return pl.pallas_call(
+    held = pl.pallas_call(
         body,
         out_shape=(
             jax.ShapeDtypeStruct(cotangent.shape, jnp.bfloat16),
             jax.ShapeDtypeStruct((width, hidden), jnp.float32),
             jax.ShapeDtypeStruct((width, hidden), jnp.float32),
         ),
-        in_specs=[vmem, anywhere, anywhere, vmem, smem, vmem, vmem],
+        in_specs=[hbm] * 7,
         out_specs=(vmem, vmem, vmem),
         scratch_shapes=scratch,
         compiler_params=pltpu.CompilerParams(
-            collective_id=0, has_side_effects=True, vmem_limit_bytes=32 * 1024 * 1024
+            collective_id=0, has_side_effects=True, vmem_limit_bytes=64 * 1024 * 1024
         ),
         name="sage_layer",
     )(
@@ -332,6 +367,14 @@
         jnp.transpose(neighbor_slots),
         neighbor_counts.reshape(1, dst_nodes),
     )
+    return pl.pallas_call(
+        write_results,
+        out_shape=tuple(jax.ShapeDtypeStruct(x.shape, x.dtype) for x in held),
+        in_specs=[vmem] * 3,
+        out_specs=(hbm, hbm, hbm),
+        scratch_shapes=[dma((3,))],
+        name="write_results",
+    )(*held)
 
 
 def solution(mesh):

time: 42.5 us -> 35.7 us (0.84)
  local copies, waits for them, and re-layouts: 8.14 us -> 0 us
  Pallas kernels: 33.3 us -> 34.9 us
    unnamed x17 -> x0, local copies, waits for them, and re-layouts: 8.14 us -> none
    pallas_call x0 -> x1, Pallas kernels: none -> 1.6 us  [on_device(): pl.pallas_call(write_results, out_shape=tuple((jax.ShapeDtypeStruct(x.sha...]
where the time goes in v2:
time: 35.7 us; the launch traced here: 35.5 us
  Pallas kernels  34.9 us (98%)
  between operations  0.64 us (2%)
    pallas_call x1, Pallas kernels, on_device(): pl.pallas_call(body, out_shape=(jax.ShapeDtypeStruct(cotangent.shape, jnp...  33.3 us
    pallas_call x1, Pallas kernels, on_device(): pl.pallas_call(write_results, out_shape=tuple((jax.ShapeDtypeStruct(x.sha...  1.6 us

profile of v2, /device:TPU:0, one launch (start us, length us, event | category | flops | bytes accessed | tf_op | source)
XLA Modules:
  0.0 35.5 jit_solution(11955656287521847627)
XLA Ops:
  0.6 33.3 %sage_layer.1 = (bf16[128,256]{1,0:T(8,128)(2,1)}, f32[64,256]{1,0:T(8,128)}, f32[64,256]{1,0:T(8,128)}) custom-call(bf16[64,4096]{1,0:T(8,128)(2,1)} %feat_hbm.1, bf16[1024,256]{1,0:T(8,128)(2,1)} %ws_hbm.1, bf16[1024,256]{1,0:T(8,128)(2,1)} %wn_hbm.1, bf16[128,256]{1,0:T(8,128)(2,1)} %cot_hbm.1, s32[16,16]{1,0:T(8,128)} %tiles_hbm.1, s32[10,2048]{1,0:T(8,128)} %bitcast.2, ...), custom_call_target="tpu_custom_call" | custom-call | tf_op jit(solution)/shard_map/sage_layer/pallas_call | solution.py:347
  33.9 1.6 %write_results.1 = (bf16[128,256]{1,0:T(8,128)(2,1)}, f32[64,256]{1,0:T(8,128)}, f32[64,256]{1,0:T(8,128)}) custom-call(bf16[128,256]{1,0:T(8,128)(2,1)} %get-tuple-element.6.a_ref, f32[64,256]{1,0:T(8,128)} %get-tuple-element.7.b_ref, f32[64,256]{1,0:T(8,128)} %get-tuple-element.8.c_ref), custom_call_target="tpu_custom_call" | custom-call | tf_op jit(solution)/shard_map/write_results/pallas_call | solution.py:370

commit v3 on v2

--- a/solution.py
+++ b/solution.py
@@ -9,6 +9,7 @@
 
 TILE = 128
 SUB = 16
+UNROLL = 16
 MESH = pl.DeviceIdType.MESH
 
 
@@ -17,8 +18,15 @@
         body(i)
         return carry
 
-    if hi > lo:
+    if hi - lo <= UNROLL:
+        for i in range(lo, hi):
+            body(i)
+    else:
         lax.fori_loop(lo, hi, step, 0)
+
+
+def wrap(i, n):
+    return jnp.where(i >= n, i - n, i)
 
 
 def grid_of(n):
@@ -97,7 +105,7 @@
 
     def greet(o):
         pl.semaphore_signal(
-            barrier, inc=1, device_id={"feat": lax.rem(me + o, n)}, device_id_type=MESH
+            barrier, inc=1, device_id={"feat": wrap(me + o, n)}, device_id_type=MESH
         )
 
     loop(1, n, greet)
@@ -115,7 +123,7 @@
     pl.semaphore_wait(barrier, n - 1)
 
     def self_copy(o):
-        to = lax.rem(me + o, n)
+        to = wrap(me + o, n)
         return pltpu.make_async_remote_copy(
             src_ref=feat_tiles.at[to],
             dst_ref=got_self.at[me],
@@ -126,7 +134,7 @@
         )
 
     def mean_copy(o):
-        to = lax.rem(me + o, n)
+        to = wrap(me + o, n)
         return pltpu.make_async_remote_copy(
             src_ref=mean_buf.at[to],
             dst_ref=got_mean.at[me],
@@ -181,11 +189,11 @@
         return (summed * scale).astype(jnp.bfloat16).astype(wire)
 
     def aggregate(o):
-        to = lax.rem(me + o, n)
+        to = wrap(me + o, n)
         mean_buf[to] = mean_of(to)
         mean_copy(o).start()
 
-    loop(1, n, aggregate)
+    lax.fori_loop(1, n, lambda o, carry: (aggregate(o), carry)[1], 0)
     mine = mean_of(me)
     mean_buf[me] = mine
     got_mean[me] = mine
@@ -211,7 +219,7 @@
         return (l * rows + r) * 2 + c
 
     def block(dl, dr, c):
-        return index(lax.rem(line - dl + lines, lines), lax.rem(row - dr + rows, rows), c)
+        return index(wrap(line - dl + lines, lines), wrap(row - dr + rows, rows), c)
 
     def pass_on(slot, to, send, recv):
         return pltpu.make_async_remote_copy(
@@ -224,11 +232,11 @@
         )
 
     def line_copy(dl, slot):
-        to = index(lax.rem(line + dl, lines), row, core)
+        to = index(wrap(line + dl, lines), row, core)
         return pass_on(slot, to, line_send.at[dl], line_recv.at[dl])
 
     def row_copy(dl, dr, slot):
-        to = index(line, lax.rem(row + dr, rows), core)
+        to = index(line, wrap(row + dr, rows), core)
         k = dl * rows + dr
         return pass_on(slot, to, row_send.at[k], row_recv.at[k])
 

time: 35.7 us -> 35.1 us (0.983)
  Pallas kernels: 34.9 us -> 34.1 us
    pallas_call x1, Pallas kernels: 33.3 us -> 32.5 us  [on_device(): pl.pallas_call(body, out_shape=(jax.ShapeDtypeStruct(cotangent.shape, jnp...]
where the time goes in v3:
time: 35.1 us; the launch traced here: 34.8 us
  Pallas kernels  34.1 us (97%)
  between operations  0.64 us (2%)
    pallas_call x1, Pallas kernels, on_device(): pl.pallas_call(body, out_shape=(jax.ShapeDtypeStruct(cotangent.shape, jnp...  32.5 us
    pallas_call x1, Pallas kernels, on_device(): pl.pallas_call(write_results, out_shape=tuple((jax.ShapeDtypeStruct(x.sha...  1.6 us

profile of v3, /device:TPU:0, one launch (start us, length us, event | category | flops | bytes accessed | tf_op | source)
XLA Modules:
  0.0 34.8 jit_solution(4273639611315987818)
XLA Ops:
  0.6 32.5 %sage_layer.1 = (bf16[128,256]{1,0:T(8,128)(2,1)}, f32[64,256]{1,0:T(8,128)}, f32[64,256]{1,0:T(8,128)}) custom-call(bf16[64,4096]{1,0:T(8,128)(2,1)} %feat_hbm.1, bf16[1024,256]{1,0:T(8,128)(2,1)} %ws_hbm.1, bf16[1024,256]{1,0:T(8,128)(2,1)} %wn_hbm.1, bf16[128,256]{1,0:T(8,128)(2,1)} %cot_hbm.1, s32[16,16]{1,0:T(8,128)} %tiles_hbm.1, s32[10,2048]{1,0:T(8,128)} %bitcast.2, ...), custom_call_target="tpu_custom_call" | custom-call | tf_op jit(solution)/shard_map/sage_layer/pallas_call | solution.py:355
  33.2 1.6 %write_results.1 = (bf16[128,256]{1,0:T(8,128)(2,1)}, f32[64,256]{1,0:T(8,128)}, f32[64,256]{1,0:T(8,128)}) custom-call(bf16[128,256]{1,0:T(8,128)(2,1)} %get-tuple-element.6.a_ref, f32[64,256]{1,0:T(8,128)} %get-tuple-element.7.b_ref, f32[64,256]{1,0:T(8,128)} %get-tuple-element.8.c_ref), custom_call_target="tpu_custom_call" | custom-call | tf_op jit(solution)/shard_map/write_results/pallas_call | solution.py:378

commit v4 on v3

--- a/solution.py
+++ b/solution.py
@@ -117,15 +117,21 @@
         feat_tiles[t] = feat_ref[:, columns(t)].astype(wire)
 
     loads[0].wait()
-    for t in range(feat_ref.shape[1] // TILE):
-        split(t)
-    got_self[me] = feat_tiles[me]
+    straight = feat_ref.dtype == wire
+
+    def cut():
+        for t in range(feat_ref.shape[1] // TILE):
+            split(t)
+        got_self[me] = feat_tiles[me]
+
+    if not straight:
+        cut()
     pl.semaphore_wait(barrier, n - 1)
 
     def self_copy(o):
         to = wrap(me + o, n)
         return pltpu.make_async_remote_copy(
-            src_ref=feat_tiles.at[to],
+            src_ref=feat_ref.at[:, columns(to)] if straight else feat_tiles.at[to],
             dst_ref=got_self.at[me],
             send_sem=self_send.at[o],
             recv_sem=self_recv.at[o],
@@ -145,6 +151,8 @@
         )
 
     loop(1, n, lambda o: self_copy(o).start())
+    if straight:
+        cut()
     for load in loads[1:4]:
         load.wait()
 

time: 35.1 us -> 35.1 us (level)
  no operation moved by 1% of the time
where the time goes in v4:
time: 35.1 us; the launch traced here: 34.8 us
  Pallas kernels  34.1 us (97%)
  between operations  0.64 us (2%)
    pallas_call x1, Pallas kernels, on_device(): pl.pallas_call(body, out_shape=(jax.ShapeDtypeStruct(cotangent.shape, jnp...  32.5 us
    pallas_call x1, Pallas kernels, on_device(): pl.pallas_call(write_results, out_shape=tuple((jax.ShapeDtypeStruct(x.sha...  1.6 us

profile of v4, /device:TPU:0, one launch (start us, length us, event | category | flops | bytes accessed | tf_op | source)
XLA Modules:
  0.0 34.8 jit_solution(3821871563161470386)
XLA Ops:
  0.6 32.5 %sage_layer.1 = (bf16[128,256]{1,0:T(8,128)(2,1)}, f32[64,256]{1,0:T(8,128)}, f32[64,256]{1,0:T(8,128)}) custom-call(bf16[64,4096]{1,0:T(8,128)(2,1)} %feat_hbm.1, bf16[1024,256]{1,0:T(8,128)(2,1)} %ws_hbm.1, bf16[1024,256]{1,0:T(8,128)(2,1)} %wn_hbm.1, bf16[128,256]{1,0:T(8,128)(2,1)} %cot_hbm.1, s32[16,16]{1,0:T(8,128)} %tiles_hbm.1, s32[10,2048]{1,0:T(8,128)} %bitcast.2, ...), custom_call_target="tpu_custom_call" | custom-call | tf_op jit(solution)/shard_map/sage_layer/pallas_call | solution.py:363
  33.2 1.6 %write_results.1 = (bf16[128,256]{1,0:T(8,128)(2,1)}, f32[64,256]{1,0:T(8,128)}, f32[64,256]{1,0:T(8,128)}) custom-call(bf16[128,256]{1,0:T(8,128)(2,1)} %get-tuple-element.6.a_ref, f32[64,256]{1,0:T(8,128)} %get-tuple-element.7.b_ref, f32[64,256]{1,0:T(8,128)} %get-tuple-element.8.c_ref), custom_call_target="tpu_custom_call" | custom-call | tf_op jit(solution)/shard_map/write_results/pallas_call | solution.py:386
